TPU v7x, 32 devices: a whole 2x2x4 slice. The times are simulated.
32 devices in a mesh: dp: 2 (over x), fsdp: 16 (over z, y, core).
Axes of the slice: x: 2, y: 2, z: 4, core: 2. Of those that a mesh axis runs over, the one named last changes fastest.
Arguments:
- hidden: bfloat16 [64, 64, 768], P(('dp', 'fsdp')), may hold values from -6 to 6
- lengths: int32 [64], P(('dp', 'fsdp')), may hold values from 5 to 32, as said below
- features: bfloat16 [64, 257, 1408], P(('dp', 'fsdp')), may hold values from -6 to 6
- cotangent: bfloat16 [64, 64, 768], P(('dp', 'fsdp')), may hold values from -6 to 6
- self_params: bfloat16 [2363392], P('fsdp')
- cross_params: bfloat16 [3346432], P('fsdp')
- ffn_params: bfloat16 [9449472], P('fsdp')
Outputs:
- mixed: bfloat16 [64, 64, 768], P(('dp', 'fsdp'))
- hidden_grad: bfloat16 [64, 64, 768], P(('dp', 'fsdp'))
- self_grad: float32 [2363392], P('fsdp')
- cross_grad: float32 [3346432], P('fsdp')
- ffn_grad: float32 [9449472], P('fsdp')
Inputs may be any that keep to these rules, and one draw needn't show every extreme that they name: lengths lie between 5 and 32; some item of every draw has 32.
All inputs are finite; a program needn't handle non-finite values.
Results may differ from a plain program's by a relative error of at most 0.017.
Values may be sent and summed in bfloat16 or wider, within the bound.
A program may use at most 384 MiB of HBM per device.

v0:
```python
from functools import partial
import math
import jax
import jax.numpy as jnp
from jax import lax
from jax.sharding import PartitionSpec as P

D = 768
HEADS = 12
HDIM = 64
F = 3072
E = 1408
NQ = 32
EPS = 1e-06
SCALE = 0.125


def self_layout():
    return [(D, D)] * 4 + [(D,)] * 5


def cross_layout():
    return [(D, D), (E, D), (E, D), (D, D)] + [(D,)] * 5


def ffn_layout():
    return [(D, F), (F,), (F, D), (D,), (D,), (D,)] * 2


def split_flat(flat_vec, layouts):
    pieces = []
    offset = 0
    for layout in layouts:
        amount = math.prod(layout)
        pieces.append(flat_vec[offset : offset + amount].reshape(layout))
        offset = offset + amount
    return pieces


def join_flat(pieces, length):
    flat_vec = jnp.concatenate([piece.reshape(-1) for piece in pieces])
    return jnp.pad(flat_vec, (0, length - flat_vec.shape[0]))


def regroup(flat_vec):
    groups = lax.axis_size("fsdp")
    replicas = lax.axis_size("dp")
    return flat_vec.reshape(groups, replicas, -1).transpose(1, 0, 2).reshape(-1)


def matmul(left, right):
    return jnp.dot(left, right, preferred_element_type=jnp.float32)


def matmul_left(left, right):
    return lax.dot_general(
        left, right, (((0,), (0,)), ((), ())), preferred_element_type=jnp.float32
    )


def matmul_right(left, right):
    return lax.dot_general(
        left, right, (((1,), (1,)), ((), ())), preferred_element_type=jnp.float32
    )


def column_sum(values):
    return jnp.sum(values.astype(jnp.float32), 0)


def layer_norm(values, gain, shift):
    average = jnp.mean(values, -1, keepdims=True)
    centered = values - average
    variance = jnp.mean(centered * centered, -1, keepdims=True)
    return centered * lax.rsqrt(variance + EPS) * gain + shift


def norm_backward(summed, gain, shift, grad_out):
    _, norm_pull = jax.vjp(layer_norm, summed, gain.astype(jnp.float32), shift.astype(jnp.float32))
    return norm_pull(grad_out)


def heads(rows, items):
    return rows.reshape(items, -1, HEADS, HDIM)


def score_block(query, keys, mask):
    scores = jnp.einsum("iqhd,ikhd->ihqk", query, keys, preferred_element_type=jnp.float32) * SCALE
    if mask is not None:
        scores = jnp.where(mask, scores, -1e30)
    return scores


def attend(query, keys, values, mask):
    scores = score_block(query, keys, mask)
    top_sum = jax.nn.logsumexp(scores, axis=-1)
    probs = jnp.exp(scores - top_sum[..., None]).astype(jnp.bfloat16)
    context = jnp.einsum("ihqk,ikhd->iqhd", probs, values, preferred_element_type=jnp.float32)
    return (context, top_sum)


def attend_back(query, keys, values, mask, top_sum, grad_context):
    probs = jnp.exp(score_block(query, keys, mask) - top_sum[..., None])
    grad_probs = jnp.einsum(
        "iqhd,ikhd->ihqk", grad_context, values, preferred_element_type=jnp.float32
    )
    inner = jnp.sum(probs * grad_probs, -1, keepdims=True)
    grad_scores = (probs * (grad_probs - inner)).astype(jnp.bfloat16)
    grad_query = (
        jnp.einsum("ihqk,ikhd->iqhd", grad_scores, keys, preferred_element_type=jnp.float32) * SCALE
    )
    grad_keys = (
        jnp.einsum("ihqk,iqhd->ikhd", grad_scores, query, preferred_element_type=jnp.float32)
        * SCALE
    )
    grad_values = jnp.einsum(
        "ihqk,iqhd->ikhd",
        probs.astype(jnp.bfloat16),
        grad_context,
        preferred_element_type=jnp.float32,
    )
    return (grad_query, grad_keys, grad_values)


def linear_back(inputs, weight, grad_out):
    return (matmul_left(inputs, grad_out), column_sum(grad_out), matmul_right(grad_out, weight))


def ffn_forward(rows, params):
    w_in, b_in, w_out, b_out, gain, shift = params
    rows_low = rows.astype(jnp.bfloat16)
    hidden_pre = matmul(rows_low, w_in) + b_in
    activated = jax.nn.gelu(hidden_pre, approximate=True).astype(jnp.bfloat16)
    summed = rows + (matmul(activated, w_out) + b_out)
    final = layer_norm(summed, gain.astype(jnp.float32), shift.astype(jnp.float32))
    return (final, (rows_low, hidden_pre, activated, summed))


def ffn_backward(grad_out, kept, params):
    w_in, b_in, w_out, b_out, gain, shift = params
    rows_low, hidden_pre, activated, summed = kept
    grad_sum, grad_gain, grad_shift = norm_backward(summed, gain, shift, grad_out)
    grad_branch = grad_sum.astype(jnp.bfloat16)
    grad_w_out, grad_b_out, grad_act = linear_back(activated, w_out, grad_branch)
    _, gelu_pull = jax.vjp(partial(jax.nn.gelu, approximate=True), hidden_pre)
    grad_pre = gelu_pull(grad_act)[0].astype(jnp.bfloat16)
    grad_w_in, grad_b_in, grad_rows = linear_back(rows_low, w_in, grad_pre)
    return (
        grad_sum + grad_rows,
        [grad_w_in, grad_b_in, grad_w_out, grad_b_out, grad_gain, grad_shift],
    )


def per_device(hidden, lengths, features, cotangent, self_params, cross_params, ffn_params):
    items, seq, width = hidden.shape
    self_full = lax.all_gather(self_params, "fsdp", axis=0, tiled=True)
    self_parts = split_flat(self_full, self_layout())
    w_q, w_k, w_v, w_o, b_q, b_v, b_o, gain_one, shift_one = self_parts
    positions = jnp.arange(seq)
    rows_at = positions[:, None]
    cols_at = positions[None, :]
    allowed = (cols_at < NQ)[None] | ((rows_at >= NQ) & (cols_at <= rows_at))[None] & (
        cols_at[None] < NQ + lengths[:, None, None]
    )
    allowed = allowed[:, None]
    inputs = hidden.reshape(-1, width)
    query_low = (matmul(inputs, w_q) + b_q).astype(jnp.bfloat16)
    key_low = matmul(inputs, w_k).astype(jnp.bfloat16)
    value_low = (matmul(inputs, w_v) + b_v).astype(jnp.bfloat16)
    context, self_top = attend(
        heads(query_low, items), heads(key_low, items), heads(value_low, items), allowed
    )
    context_low = context.reshape(-1, width).astype(jnp.bfloat16)
    summed_one = inputs.astype(jnp.float32) + (matmul(context_low, w_o) + b_o)
    first = layer_norm(summed_one, gain_one.astype(jnp.float32), shift_one.astype(jnp.float32))
    first_items = first.reshape(items, seq, width)
    query_rows = first_items[:, :NQ].reshape(-1, width)
    text_rows = first_items[:, NQ:].reshape(-1, width)
    cross_full = lax.all_gather(cross_params, "fsdp", axis=0, tiled=True)
    cross_parts = split_flat(cross_full, cross_layout())
    cross_wq, cross_wk, cross_wv, cross_wo, cross_bq, cross_bv, cross_bo, gain_two, shift_two = (
        cross_parts
    )
    query_in = query_rows.astype(jnp.bfloat16)
    image_rows = features.reshape(-1, features.shape[-1])
    cross_query = (matmul(query_in, cross_wq) + cross_bq).astype(jnp.bfloat16)
    cross_key = matmul(image_rows, cross_wk).astype(jnp.bfloat16)
    cross_value = (matmul(image_rows, cross_wv) + cross_bv).astype(jnp.bfloat16)
    cross_context, cross_top = attend(
        heads(cross_query, items), heads(cross_key, items), heads(cross_value, items), None
    )
    cross_low = cross_context.reshape(-1, width).astype(jnp.bfloat16)
    summed_two = query_rows + (matmul(cross_low, cross_wo) + cross_bo)
    second = layer_norm(summed_two, gain_two.astype(jnp.float32), shift_two.astype(jnp.float32))
    ffn_full = lax.all_gather(ffn_params, "fsdp", axis=0, tiled=True)
    ffn_parts = split_flat(ffn_full, ffn_layout())
    query_final, query_kept = ffn_forward(second, ffn_parts[:6])
    text_final, text_kept = ffn_forward(text_rows, ffn_parts[6:])
    mixed = jnp.concatenate(
        [query_final.reshape(items, NQ, width), text_final.reshape(items, -1, width)], 1
    ).astype(jnp.bfloat16)
    grad_items = cotangent.astype(jnp.float32)
    grad_query_final = grad_items[:, :NQ].reshape(-1, width)
    grad_text_final = grad_items[:, NQ:].reshape(-1, width)
    ffn_back = split_flat(lax.all_gather(ffn_params, "fsdp", axis=0, tiled=True), ffn_layout())
    grad_second, query_grads = ffn_backward(grad_query_final, query_kept, ffn_back[:6])
    grad_text, text_grads = ffn_backward(grad_text_final, text_kept, ffn_back[6:])
    ffn_flat_grad = join_flat(query_grads + text_grads, ffn_full.shape[0])
    ffn_grad = lax.psum_scatter(
        regroup(ffn_flat_grad), ("dp", "fsdp"), scatter_dimension=0, tiled=True
    )
    cross_back = split_flat(
        lax.all_gather(cross_params, "fsdp", axis=0, tiled=True), cross_layout()
    )
    grad_summed_two, grad_gain_two, grad_shift_two = norm_backward(
        summed_two, cross_back[7], cross_back[8], grad_second
    )
    grad_cross_out = grad_summed_two.astype(jnp.bfloat16)
    grad_cross_wo, grad_cross_bo, grad_cross_ctx = linear_back(
        cross_low, cross_back[3], grad_cross_out
    )
    grad_cq, grad_ck, grad_cv = attend_back(
        heads(cross_query, items),
        heads(cross_key, items),
        heads(cross_value, items),
        None,
        cross_top,
        heads(grad_cross_ctx.astype(jnp.bfloat16), items),
    )
    grad_cq = grad_cq.reshape(-1, width).astype(jnp.bfloat16)
    grad_ck = grad_ck.reshape(-1, width).astype(jnp.bfloat16)
    grad_cv = grad_cv.reshape(-1, width).astype(jnp.bfloat16)
    grad_cross_wq, grad_cross_bq, grad_query_in = linear_back(query_in, cross_back[0], grad_cq)
    grad_cross_wk = matmul_left(image_rows, grad_ck)
    grad_cross_wv = matmul_left(image_rows, grad_cv)
    grad_cross_bv = column_sum(grad_cv)
    grad_query_rows = grad_summed_two + grad_query_in
    cross_list = [
        grad_cross_wq,
        grad_cross_wk,
        grad_cross_wv,
        grad_cross_wo,
        grad_cross_bq,
        grad_cross_bv,
        grad_cross_bo,
        grad_gain_two,
        grad_shift_two,
    ]
    cross_flat_grad = join_flat(cross_list, cross_full.shape[0])
    cross_grad = lax.psum_scatter(
        regroup(cross_flat_grad), ("dp", "fsdp"), scatter_dimension=0, tiled=True
    )
    self_back = split_flat(lax.all_gather(self_params, "fsdp", axis=0, tiled=True), self_layout())
    grad_first = jnp.concatenate(
        [grad_query_rows.reshape(items, NQ, width), grad_text.reshape(items, -1, width)], 1
    ).reshape(-1, width)
    grad_summed_one, grad_gain_one, grad_shift_one = norm_backward(
        summed_one, self_back[7], self_back[8], grad_first
    )
    grad_attn = grad_summed_one.astype(jnp.bfloat16)
    grad_w_o, grad_b_o, grad_ctx = linear_back(context_low, self_back[3], grad_attn)
    grad_q, grad_k, grad_v = attend_back(
        heads(query_low, items),
        heads(key_low, items),
        heads(value_low, items),
        allowed,
        self_top,
        heads(grad_ctx.astype(jnp.bfloat16), items),
    )
    grad_q = grad_q.reshape(-1, width).astype(jnp.bfloat16)
    grad_k = grad_k.reshape(-1, width).astype(jnp.bfloat16)
    grad_v = grad_v.reshape(-1, width).astype(jnp.bfloat16)
    grad_w_q, grad_b_q, input_from_q = linear_back(inputs, self_back[0], grad_q)
    grad_w_k = matmul_left(inputs, grad_k)
    input_from_k = matmul_right(grad_k, self_back[1])
    grad_w_v, grad_b_v, input_from_v = linear_back(inputs, self_back[2], grad_v)
    hidden_grad = (
        (grad_summed_one + input_from_q + input_from_k + input_from_v)
        .reshape(items, seq, width)
        .astype(jnp.bfloat16)
    )
    self_list = [
        grad_w_q,
        grad_w_k,
        grad_w_v,
        grad_w_o,
        grad_b_q,
        grad_b_v,
        grad_b_o,
        grad_gain_one,
        grad_shift_one,
    ]
    self_flat_grad = join_flat(self_list, self_full.shape[0])
    self_grad = lax.psum_scatter(
        regroup(self_flat_grad), ("dp", "fsdp"), scatter_dimension=0, tiled=True
    )
    self_grad, cross_grad, ffn_grad = (
        lax.all_gather(self_grad.astype(jnp.bfloat16), "dp", axis=0, tiled=True).astype(
            self_grad.dtype
        ),
        lax.all_gather(cross_grad.astype(jnp.bfloat16), "dp", axis=0, tiled=True).astype(
            cross_grad.dtype
        ),
        lax.all_gather(ffn_grad.astype(jnp.bfloat16), "dp", axis=0, tiled=True).astype(
            ffn_grad.dtype
        ),
    )
    return (mixed, hidden_grad, self_grad, cross_grad, ffn_grad)


def solution(mesh):
    return jax.shard_map(
        per_device,
        mesh=mesh,
        in_specs=(
            P(("dp", "fsdp"), None, None),
            P(("dp", "fsdp")),
            P(("dp", "fsdp"), None, None),
            P(("dp", "fsdp"), None, None),
            P("fsdp"),
            P("fsdp"),
            P("fsdp"),
        ),
        out_specs=(
            P(("dp", "fsdp"), None, None),
            P(("dp", "fsdp"), None, None),
            P("fsdp"),
            P("fsdp"),
            P("fsdp"),
        ),
        check_vma=False,
    )
```

profile of v0, /device:TPU:0, one launch (start us, length us, event | category | flops | bytes accessed | tf_op | source)
XLA Modules:
  0.0 2604.6 jit_solution(10896527017699016095)
XLA Ops:
  17.5 14.2 reshape.500
  35.5 60.6 %all-gather.11.cloned.1.call-done = bf16[16,1,147712]{2,1,0:T(2,128)(2,1)} async-done(((bf16[1,1,147712]{2,1,0:T(2,128)(2,1)}), bf16[16,1,147712]{2,1,0:T(2,128)(2,1)}) %all-gather.11.cloned.1.call-update) | async-done | bytes 4726800 | tf_op jit(solution)/shard_map/all_gather | solution.py:156
  96.1 78.1 %reduce.11 = bf16[16,147712]{1,0:T(8,128)(2,1)} reduce(bf16[16,1,147712]{2,1,0:T(2,128)(2,1)} %all-gather.11.cloned.1.call-done, bf16[]{:T(256)} %constant.79), dimensions={1}, to_apply=%all-gather.reduce_sub_computation | reduce | bytes 9453570 | tf_op jit(solution)/shard_map/all_gather | solution.py:156
  174.2 10.1 reshape.497
  209.2 141.5 %reduce.12 = bf16[16,209152]{1,0:T(8,128)(2,1)} reduce(bf16[16,1,209152]{2,1,0:T(2,128)(2,1)} %all-gather.13.cloned.1.call-done, bf16[]{:T(256)} %constant.79), dimensions={1}, to_apply=%all-gather.1.reduce_sub_computation | reduce | bytes 13385730 | tf_op jit(solution)/shard_map/all_gather | solution.py:179
  350.8 14.0 reshape.499
  420.2 400.6 %reduce.13 = bf16[16,590592]{1,0:T(8,128)(2,1)} reduce(bf16[16,1,590592]{2,1,0:T(2,128)(2,1)} %all-gather.15.cloned.1.call-done, bf16[]{:T(256)} %constant.79), dimensions={1}, to_apply=%all-gather.2.reduce_sub_computation | reduce | bytes 37797888 | tf_op jit(solution)/shard_map/all_gather | solution.py:195
  820.8 43.1 %reshape.501 = bf16[9449472]{0:T(1024)(128)(2,1)} reshape(bf16[16,590592]{1,0:T(8,128)(2,1)} %reduce.13) | data formatting | bytes 37797888
  863.9 14.0 fusion.71
  880.7 8.2 slice.166
  888.9 9.2 slice.169
  913.7 9.3 slice.177
  1038.7 8.6 pad.12
  1047.3 10.3 reshape.482
  1138.5 10.0 pad.13
  1148.6 13.4 reshape.488
  1162.0 10.4 copy.156
  1172.4 9.8 reshape.489
  1192.0 10.8 reshape.491
  1210.0 10.8 reshape.493
  1221.4 8.3 constant_dynamic-update-slice_fusion.6
  1233.6 80.5 %dynamic-update-slice.6 = f32[9447936]{0:T(1024)} dynamic-update-slice(f32[9447936]{0:T(1024)} %constant_dynamic-update-slice_fusion.25, f32[2359296]{0:T(1024)} %bitcast.168, s32[]{} %constant.91) | dynamic-update-slice | bytes 18874372
  1315.4 80.5 %dynamic-update-slice.8 = f32[9447936]{0:T(1024)} dynamic-update-slice(f32[9447936]{0:T(1024)} %constant_dynamic-update-slice_fusion.24, f32[2359296]{0:T(1024)} %reshape.493, s32[]{} %constant.93) | dynamic-update-slice | bytes 18874372
  1399.8 27.1 %pad.14 = f32[9449472]{0:T(1024)} pad(f32[9447936]{0:T(1024)} %constant_dynamic-update-slice_fusion.21, f32[]{:T(128)} %constant.23.clone.1), padding=0_1536 | pad | bytes 75589632 | tf_op jit(solution)/shard_map/jit(_pad)/pad | solution.py:42
  1426.9 59.6 %reshape.494 = f32[16,2,295296]{2,1,0:T(2,128)} reshape(f32[9449472]{0:T(1024)} %pad.14) | data formatting | bytes 75595776 | tf_op jit(solution)/shard_map/reshape | solution.py:48
  1486.5 29.9 %copy.157 = f32[2,16,295296]{2,1,0:T(8,128)} copy(f32[2,16,295296]{2,0,1:T(2,128)} %bitcast.161) | data formatting | bytes 75595776 | tf_op jit(solution)/shard_map/transpose | solution.py:48
  1516.4 31.6 %reshape.495 = f32[9449472]{0:T(1024)} reshape(f32[2,16,295296]{2,1,0:T(8,128)} %copy.157) | data formatting | bytes 75595776 | tf_op jit(solution)/shard_map/reshape | solution.py:48
  1548.0 960.9 %all-reduce.8 = (bf16[2363392]{0:T(1024)(128)(2,1)}, bf16[3346432]{0:T(1024)(128)(2,1)}, bf16[9449472]{0:T(1024)(128)(2,1)}) all-reduce(f32[2363392]{0:T(1024)} %reshape.483, f32[3346432]{0:T(1024)} %reshape.489, f32[9449472]{0:T(1024)} %reshape.495), channel_id=2, replica_groups=mesh['dp'=2,'fsdp'=16] {'dp','fsdp'}, use_global_device_ids=true, to_apply=%region_28.29.clone | all-reduce | flops 15159296 | bytes 90955776
  2510.1 8.6 all-gather.3
  2531.3 14.9 all-gather.4
  2557.1 10.7 all-gather.17.cloned.1.call-done
  2567.8 26.9 %convert_reduce_fusion = f32[2,295296]{1,0:T(2,128)S(1)} fusion(bf16[2,1,295296]{2,1,0:T(2,128)(2,1)} %all-gather.17.cloned.1.call-done), kind=kLoop, calls=%fused_computation.6 | loop fusion | flops 590592 | bytes 3543552 | tf_op jit(solution)/shard_map/convert_element_type | solution.py:304
  (488 shorter events, 362.6 us)
Async XLA Ops:
  7.2 10.3 copy-start.56
  7.2 88.9 %all-gather.11.cloned.1.call-start = ((), (), s32[]{:S(2)}) async-start(), calls=%async_computation | async-start | bytes 10044416 | tf_op jit(solution)/shard_map/all_gather | solution.py:156
  11.7 197.5 %all-gather.13.cloned.1.call-start = ((), (), s32[]{:S(2)}) async-start(), calls=%async_computation.1 | async-start | bytes 14222336 | tf_op jit(solution)/shard_map/all_gather | solution.py:179
  17.4 14.4 copy-start.34
  17.4 402.8 %all-gather.15.cloned.1.call-start = ((), (), s32[]{:S(2)}) async-start(), calls=%async_computation.2 | async-start | bytes 40160256 | tf_op jit(solution)/shard_map/all_gather | solution.py:195
  31.7 2536.1 %all-gather.17.cloned.1.call-start = ((), (), s32[]{:S(2)}) async-start(), calls=%async_computation.3 | async-start | bytes 3543552 | tf_op jit(solution)/shard_map/all_gather | solution.py:304
  204.9 145.9 %copy-start.7 = (bf16[768,768]{1,0:T(8,128)(2,1)}, bf16[768,768]{1,0:T(8,128)(2,1)S(1)}, u32[]{:S(2)}) copy-start(bf16[768,768]{1,0:T(8,128)(2,1)S(1)} %reshape.456) | copy-start | bytes 3538948
  207.8 143.0 %copy-start.44 = (f32[2,32,768]{2,1,0:T(8,128)}, f32[2,32,768]{2,1,0:T(8,128)S(1)}, u32[]{:S(2)}) copy-start(f32[2,32,768]{2,1,0:T(8,128)S(1)} %get-tuple-element.72) | copy-start | bytes 589828
  208.6 196.8 %copy-start.59 = (bf16[2,32,768]{2,1,0:T(8,128)(2,1)}, bf16[2,32,768]{2,1,0:T(8,128)(2,1)S(1)}, u32[]{:S(2)}) copy-start(bf16[2,32,768]{2,1,0:T(8,128)(2,1)S(1)} %get-tuple-element.69) | copy-start | bytes 294916
  898.2 12.2 slice-start.2
  901.8 8.5 slice-start.3
  992.6 12.9 copy-start.40
  994.2 19.5 copy-start.46
  1031.3 6.8 copy-start.95
  1031.3 6.8 copy-start.96
  1131.2 6.8 copy-start.106
  1192.0 10.8 copy-start.51
  1192.0 10.8 copy-start.64
  1210.0 10.8 copy-start.113
  1221.4 8.3 copy-start.103
  1221.4 9.6 copy-start.102
  1221.4 11.0 copy-start.101
  1233.6 80.5 %copy-start.114 = (f32[3072]{0:T(1024)S(1)}, f32[3072]{0:T(1024)}, u32[]{:S(2)}) copy-start(f32[3072]{0:T(1024)} %get-tuple-element.21) | copy-start | bytes 36868
  1315.4 80.5 %copy-start.105 = (f32[768]{0:T(1024)S(1)}, f32[768]{0:T(1024)}, u32[]{:S(2)}) copy-start(f32[768]{0:T(1024)} %get-tuple-element.19) | copy-start | bytes 9220
  1315.4 81.8 %copy-start.104 = (f32[768]{0:T(1024)S(1)}, f32[768]{0:T(1024)}, u32[]{:S(2)}) copy-start(f32[768]{0:T(1024)} %get-tuple-element.7) | copy-start | bytes 9220
  1315.4 83.1 %copy-start.100 = (f32[768]{0:T(1024)S(1)}, f32[768]{0:T(1024)}, u32[]{:S(2)}) copy-start(f32[768]{0:T(1024)} %get-tuple-element.13) | copy-start | bytes 9220
  2546.2 8.5 copy-start.4
  2546.2 8.5 copy-start.30
  2546.2 8.5 copy-start.39
  2546.2 8.5 copy-start.122
  2547.5 6.5 copy-start.75
  2547.5 6.5 copy-start.76
  (107 other events, 326.7 us)
Sparse Core Ops, SparseCore 0:
  11.8 84.2 all-gather.10
  98.9 103.9 all-gather.12
  205.1 186.1 all-gather.14
  2531.4 36.2 all-gather.16
where the time goes:
time: 2630 us; the launch traced here: 2600 us
  blocking collectives  984 us (37%)
  local copies, waits for them, and re-layouts  767 us (29%)
  other arithmetic  672 us (26%)
  matrix products  94.1 us (4%)
  waiting for transfers between devices  71.3 us (3%)
    unnamed x1, blocking collectives  961 us
    all_gather x1, other arithmetic, per_device(): ffn_full = lax.all_gather(ffn_params, 'fsdp', axis=0, tiled=True)  401 us
    unnamed x312, local copies, waits for them, and re-layouts  337 us
    all_gather x1, other arithmetic, per_device(): cross_full = lax.all_gather(cross_params, 'fsdp', axis=0, tiled=True)  142 us
    reshape x6, local copies, waits for them, and re-layouts, regroup(): return flat_vec.reshape(groups, replicas, -1).transpose(1, 0, 2).reshape(-1)  133 us
    all_gather x1, other arithmetic, per_device(): self_full = lax.all_gather(self_params, 'fsdp', axis=0, tiled=True)  78.1 us
    all_gather x1, waiting for transfers between devices, per_device(): self_full = lax.all_gather(self_params, 'fsdp', axis=0, tiled=True)  60.6 us
  transfers between devices with their start and end apart: 4, of which 2 were waited for; matrix products, arithmetic and copies ran while one was open for 14% of the time, Pallas kernels for 0%

commit v1 on v0

--- a/solution.py
+++ b/solution.py
@@ -13,6 +13,18 @@
 NQ = 32
 EPS = 1e-06
 SCALE = 0.125
+
+
+def doubled_up(x, axis, dim):
+    ways, here = (lax.axis_size(axis), lax.axis_index(axis))
+    grown, reach = (x, 1)
+    while reach < ways:
+        theirs = lax.ppermute(grown, axis, [(d, d ^ reach) for d in range(ways)])
+        mine_first = jnp.concatenate([grown, theirs], axis=dim)
+        theirs_first = jnp.concatenate([theirs, grown], axis=dim)
+        grown = jnp.where(here & reach == 0, mine_first, theirs_first)
+        reach = 2 * reach
+    return grown
 
 
 def self_layout():
@@ -176,7 +188,7 @@
     first_items = first.reshape(items, seq, width)
     query_rows = first_items[:, :NQ].reshape(-1, width)
     text_rows = first_items[:, NQ:].reshape(-1, width)
-    cross_full = lax.all_gather(cross_params, "fsdp", axis=0, tiled=True)
+    cross_full = doubled_up(cross_params, "fsdp", 0)
     cross_parts = split_flat(cross_full, cross_layout())
     cross_wq, cross_wk, cross_wv, cross_wo, cross_bq, cross_bv, cross_bo, gain_two, shift_two = (
         cross_parts

time: 2630 us -> 2940 us (1.12)
  waiting for transfers between devices: 71.3 us -> 317 us
  other arithmetic: 672 us -> 713 us
    ppermute x0 -> x4, waiting for transfers between devices: none -> 311 us  [doubled_up(): theirs = lax.ppermute(grown, axis, [(d, d ^ reach) for d in range(ways)])]
    all_gather x1, waiting for transfers between devices: 60.6 us -> 0.01 us  [per_device(): self_full = lax.all_gather(self_params, 'fsdp', axis=0, tiled=True)]
    select_n x0 -> x4, other arithmetic: none -> 33.8 us  [doubled_up(): grown = jnp.where(here & reach == 0, mine_first, theirs_first)]
    unnamed x312 -> x290, local copies, waits for them, and re-layouts: 337 us -> 340 us
  transfers between devices with their start and end apart: 4 -> 8, of which waited for: 2 -> 5; matrix products, arithmetic and copies ran while one was open for 14% -> 14% of each run, Pallas kernels for 0% -> 0%
where the time goes in v1:
time: 2940 us; the launch traced here: 2920 us
  blocking collectives  980 us (33%)
  local copies, waits for them, and re-layouts  790 us (27%)
  other arithmetic  713 us (24%)
  waiting for transfers between devices  317 us (11%)
  matrix products  96.1 us (3%)
    unnamed x1, blocking collectives  955 us
    all_gather x1, other arithmetic, per_device(): ffn_full = lax.all_gather(ffn_params, 'fsdp', axis=0, tiled=True)  401 us
    unnamed x290, local copies, waits for them, and re-layouts  340 us
    ppermute x4, waiting for transfers between devices, doubled_up(): theirs = lax.ppermute(grown, axis, [(d, d ^ reach) for d in range(ways)])  311 us
    all_gather x1, other arithmetic, per_device(): lax.all_gather(cross_params, 'fsdp', axis=0, tiled=True)  142 us
    reshape x6, local copies, waits for them, and re-layouts, regroup(): return flat_vec.reshape(groups, replicas, -1).transpose(1, 0, 2).reshape(-1)  132 us
    all_gather x1, other arithmetic, per_device(): self_full = lax.all_gather(self_params, 'fsdp', axis=0, tiled=True)  77.5 us
  transfers between devices with their start and end apart: 8, of which 5 were waited for; matrix products, arithmetic and copies ran while one was open for 14% of the time, Pallas kernels for 0%

profile of v1, /device:TPU:0, one launch (start us, length us, event | category | flops | bytes accessed | tf_op | source)
XLA Modules:
  0.0 2918.3 jit_solution(11994993512006377959)
XLA Ops:
  18.3 19.1 collective-permute-done.1
  46.7 77.1 %collective-permute-done.2 = bf16[836608]{0:T(1024)(128)(2,1)} collective-permute-done((bf16[836608]{0:T(1024)(128)(2,1)S(1)}, bf16[836608]{0:T(1024)(128)(2,1)}, u32[]{:S(2)}, u32[]{:S(2)}) %collective-permute-start.2) | collective-permute-done | bytes 1673248 | tf_op jit(solution)/shard_map/ppermute | solution.py:22
  130.0 14.2 reshape.505
  154.2 212.8 %collective-permute-done.3 = bf16[1673216]{0:T(1024)(128)(2,1)} collective-permute-done((bf16[1673216]{0:T(1024)(128)(2,1)S(1)}, bf16[1673216]{0:T(1024)(128)(2,1)}, u32[]{:S(2)}, u32[]{:S(2)}) %collective-permute-start.3) | collective-permute-done | bytes 3346464 | tf_op jit(solution)/shard_map/ppermute | solution.py:22
  367.0 24.8 maximum_select_fusion
  429.9 77.5 %reduce.11 = bf16[16,147712]{1,0:T(8,128)(2,1)} reduce(bf16[16,1,147712]{2,1,0:T(2,128)(2,1)} %all-gather.11.cloned.1.call-done, bf16[]{:T(256)} %constant.92), dimensions={1}, to_apply=%all-gather.reduce_sub_computation | reduce | bytes 9453570 | tf_op jit(solution)/shard_map/all_gather | solution.py:168
  507.4 10.4 reshape.504
  564.1 141.5 %reduce.13 = bf16[16,209152]{1,0:T(8,128)(2,1)} reduce(bf16[16,1,209152]{2,1,0:T(2,128)(2,1)} %all-gather.15.cloned.1.call-done, bf16[]{:T(256)} %constant.92), dimensions={1}, to_apply=%all-gather.2.reduce_sub_computation | reduce | bytes 13385730 | tf_op jit(solution)/shard_map/all_gather | solution.py:225
  705.6 13.7 reshape.508
  730.5 400.9 %reduce.12 = bf16[16,590592]{1,0:T(8,128)(2,1)} reduce(bf16[16,1,590592]{2,1,0:T(2,128)(2,1)} %all-gather.13.cloned.1.call-done, bf16[]{:T(256)} %constant.92), dimensions={1}, to_apply=%all-gather.1.reduce_sub_computation | reduce | bytes 37797888 | tf_op jit(solution)/shard_map/all_gather | solution.py:207
  1131.3 43.2 %reshape.506 = bf16[9449472]{0:T(1024)(128)(2,1)} reshape(bf16[16,590592]{1,0:T(8,128)(2,1)} %reduce.12) | data formatting | bytes 37797888
  1174.5 14.1 fusion.73
  1199.5 9.3 slice.175
  1222.0 9.3 slice.183
  1354.2 8.7 pad.12
  1362.9 10.3 reshape.489
  1457.0 10.1 pad.13
  1467.0 13.3 reshape.495
  1480.4 10.4 copy.156
  1490.8 10.0 reshape.496
  1510.4 10.8 reshape.498
  1528.3 10.8 reshape.500
  1551.9 80.4 %dynamic-update-slice.6 = f32[9447936]{0:T(1024)} dynamic-update-slice(f32[9447936]{0:T(1024)} %constant_dynamic-update-slice_fusion.25, f32[2359296]{0:T(1024)} %bitcast.172, s32[]{} %constant.104) | dynamic-update-slice | bytes 18874372
  1633.6 80.4 %dynamic-update-slice.8 = f32[9447936]{0:T(1024)} dynamic-update-slice(f32[9447936]{0:T(1024)} %constant_dynamic-update-slice_fusion.24, f32[2359296]{0:T(1024)} %reshape.500, s32[]{} %constant.106) | dynamic-update-slice | bytes 18874372
  1717.9 27.0 pad.14
  1744.9 59.4 %reshape.501 = f32[16,2,295296]{2,1,0:T(2,128)} reshape(f32[9449472]{0:T(1024)} %pad.14) | data formatting | bytes 75595776 | tf_op jit(solution)/shard_map/reshape | solution.py:60
  1804.4 29.9 %copy.157 = f32[2,16,295296]{2,1,0:T(8,128)} copy(f32[2,16,295296]{2,0,1:T(2,128)} %bitcast.165) | data formatting | bytes 75595776 | tf_op jit(solution)/shard_map/transpose | solution.py:60
  1834.3 31.6 %reshape.502 = f32[9449472]{0:T(1024)} reshape(f32[2,16,295296]{2,1,0:T(8,128)} %copy.157) | data formatting | bytes 75595776 | tf_op jit(solution)/shard_map/reshape | solution.py:60
  1865.9 955.3 %all-reduce.8 = (bf16[2363392]{0:T(1024)(128)(2,1)}, bf16[3346432]{0:T(1024)(128)(2,1)}, bf16[9449472]{0:T(1024)(128)(2,1)}) all-reduce(f32[2363392]{0:T(1024)} %reshape.490, f32[3346432]{0:T(1024)} %reshape.496, f32[9449472]{0:T(1024)} %reshape.502), channel_id=2, replica_groups=mesh['dp'=2,'fsdp'=16] {'dp','fsdp'}, use_global_device_ids=true, to_apply=%region_28.29.clone | all-reduce | flops 15159296 | bytes 90955776
  2822.4 8.6 all-gather.3
  2844.2 15.8 all-gather.4
  2881.1 26.9 convert_reduce_fusion
  (482 shorter events, 435.5 us)
Async XLA Ops:
  7.2 34.0 %copy-start.43 = (bf16[209152]{0:T(1024)(128)(2,1)S(1)}, bf16[209152]{0:T(1024)(128)(2,1)}, u32[]{:S(2)}) copy-start(bf16[209152]{0:T(1024)(128)(2,1)} %param.12) | copy-start | bytes 1254916
  7.2 422.7 %all-gather.11.cloned.1.call-start = ((), (), s32[]{:S(2)}) async-start(), calls=%async_computation | async-start | bytes 10044416 | tf_op jit(solution)/shard_map/all_gather | solution.py:168
  7.2 2.1 collective-permute-start
  10.9 26.5 collective-permute-start.1
  18.2 545.8 %all-gather.15.cloned.1.call-start = ((), (), s32[]{:S(2)}) async-start(), calls=%async_computation.2 | async-start | bytes 14222336 | tf_op jit(solution)/shard_map/all_gather | solution.py:225
  39.5 84.3 %collective-permute-start.2 = (bf16[836608]{0:T(1024)(128)(2,1)S(1)}, bf16[836608]{0:T(1024)(128)(2,1)}, u32[]{:S(2)}, u32[]{:S(2)}) collective-permute-start(bf16[836608]{0:T(1024)(128)(2,1)S(1)} %maximum_select_fusion.2), channel_id=1, source_target_pairs={{0,4},{1,5},{2,6},{3,7},{4,0},{5,1},{6,2},{7,3},{8,12},{9,13},{10,... | collective-permute-start | bytes 5019656 | tf_op jit(solution)/shard_map/ppermute | solution.py:22
  46.6 683.8 %all-gather.13.cloned.1.call-start = ((), (), s32[]{:S(2)}) async-start(), calls=%async_computation.1 | async-start | bytes 40160256 | tf_op jit(solution)/shard_map/all_gather | solution.py:207
  46.7 83.3 %copy-start.52 = (bf16[590592]{0:T(1024)(128)(2,1)S(1)}, bf16[590592]{0:T(1024)(128)(2,1)}, u32[]{:S(2)}) copy-start(bf16[590592]{0:T(1024)(128)(2,1)} %param.13) | copy-start | bytes 3543556
  129.2 237.8 %collective-permute-start.3 = (bf16[1673216]{0:T(1024)(128)(2,1)S(1)}, bf16[1673216]{0:T(1024)(128)(2,1)}, u32[]{:S(2)}, u32[]{:S(2)}) collective-permute-start(bf16[1673216]{0:T(1024)(128)(2,1)S(1)} %maximum_select_fusion.1), channel_id=1, source_target_pairs={{0,8},{1,9},{2,10},{3,11},{4,12},{5,13},{6,14},{7,15},{8,0},{9,1},... | collective-permute-start | bytes 10039304 | tf_op jit(solution)/shard_map/ppermute | solution.py:22
  144.2 2736.9 %all-gather.17.cloned.1.call-start = ((), (), s32[]{:S(2)}) async-start(), calls=%async_computation.3 | async-start | bytes 3543552 | tf_op jit(solution)/shard_map/all_gather | solution.py:316
  144.7 7.9 copy-start.117
  404.5 8.3 copy-start.51
  517.7 8.6 copy-start.12
  542.0 9.0 copy-start.33
  1208.8 9.8 slice-start.2
  1260.2 11.5 copy-start.7
  1305.0 9.7 copy-start.35
  1306.6 14.6 copy-start.36
  1309.8 19.5 copy-start.41
  1510.4 10.8 copy-start.47
  1510.4 10.8 copy-start.60
  1528.3 10.8 copy-start.105
  1539.7 8.3 copy-start.94
  1539.7 9.6 copy-start.93
  1539.7 10.9 copy-start.92
  1551.9 80.4 %copy-start.106 = (f32[3072]{0:T(1024)S(1)}, f32[3072]{0:T(1024)}, u32[]{:S(2)}) copy-start(f32[3072]{0:T(1024)} %get-tuple-element.21) | copy-start | bytes 36868
  1633.6 80.4 %copy-start.97 = (f32[768]{0:T(1024)S(1)}, f32[768]{0:T(1024)}, u32[]{:S(2)}) copy-start(f32[768]{0:T(1024)} %get-tuple-element.19) | copy-start | bytes 9220
  1633.6 81.7 %copy-start.95 = (f32[768]{0:T(1024)S(1)}, f32[768]{0:T(1024)}, u32[]{:S(2)}) copy-start(f32[768]{0:T(1024)} %get-tuple-element.7) | copy-start | bytes 9220
  1633.6 83.0 %copy-start.91 = (f32[768]{0:T(1024)S(1)}, f32[768]{0:T(1024)}, u32[]{:S(2)}) copy-start(f32[768]{0:T(1024)} %get-tuple-element.13) | copy-start | bytes 9220
  2844.2 26.4 copy-start.4
  2844.2 26.4 copy-start.112
  2860.0 12.3 copy-start.5
  (100 other events, 373.7 us)
Sparse Core Ops, SparseCore 0:
  18.4 106.8 all-gather.10
  128.1 207.9 all-gather.14
  338.2 197.5 all-gather.12
  2844.3 36.7 all-gather.16
